TPU v7x, 32 devices: a whole 2x2x4 slice. The times are simulated.
32 devices in a mesh: dp: 8 (over z, y), fsdp: 4 (over x, core).
Axes of the slice: x: 2, y: 2, z: 4, core: 2. Of those that a mesh axis runs over, the one named last changes fastest.
Arguments:
- student_frames: bfloat16 [16384, 1024], P(('dp', 'fsdp')), may hold values from -6 to 6
- teacher_layers: bfloat16 [2, 16384, 1024], P(None, ('dp', 'fsdp')), as said below
- mask_blocks: int32 [32, 32], P(('dp', 'fsdp')), may hold values from 0 to 63, as said below
- w_in: bfloat16 [384, 1024], P('fsdp'), may hold values from -6 to 6
- w_out: bfloat16 [384, 1024], P('fsdp'), may hold values from -6 to 6
- teacher_in: float32 [384, 1024], P('fsdp'), may hold values from -6 to 6
- teacher_out: float32 [384, 1024], P('fsdp'), may hold values from -6 to 6
Outputs:
- grad_in: float32 [384, 1024], P('fsdp')
- grad_out: float32 [384, 1024], P('fsdp')
- new_teacher_in: float32 [384, 1024], P('fsdp')
- new_teacher_out: float32 [384, 1024], P('fsdp')
Inputs may be any that keep to these rules, and one draw needn't show every extreme that they name: `mask_blocks`: each row holds 32 different block numbers. `teacher_layers`: finite values.
All inputs are finite; a program needn't handle non-finite values.
Results may differ from a plain program's by a relative error of at most 0.0029.
Values may be sent and summed in bfloat16 or wider, within the bound.
A program may use at most 64 MiB of HBM per device.

v0:
```python
import jax
import jax.numpy as jnp
from jax import lax
from jax.sharding import PartitionSpec as P

SPAN = 8


def gelu_fn(inputs):
    return jax.nn.gelu(inputs, approximate=True)


def targets_of(layers):
    values = layers.astype(jnp.float32)
    center = values - jnp.mean(values, axis=1, keepdims=True)
    spread = jnp.mean(center * center, axis=1, keepdims=True)
    return jnp.mean(center / jnp.sqrt(spread + 1e-05), axis=0)


def frame_mask(blocks, frames):
    block_of = jnp.arange(frames, dtype=jnp.int32) // SPAN
    matches = block_of[:, None] == blocks[None, :]
    return jnp.any(matches, axis=1).astype(jnp.float32)


def local_terms(frames_here, layers, blocks, full_in, full_out, total_masked):
    model_width = full_in.shape[1]
    hidden = full_in.shape[0]
    before = lax.dot_general(
        frames_here, full_in, (((1,), (1,)), ((), ())), preferred_element_type=jnp.float32
    ) * model_width ** (-0.5)
    active, pullback = jax.vjp(gelu_fn, before)
    active_low = active.astype(jnp.bfloat16)
    predicted = jnp.dot(active_low, full_out, preferred_element_type=jnp.float32) * hidden ** (-0.5)
    target = targets_of(layers)
    masked = frame_mask(blocks, frames_here.shape[0])
    scaled_error = (masked[:, None] * (predicted - target) * (hidden / total_masked) ** 0.5).astype(
        jnp.bfloat16
    )
    term_out = (
        lax.dot_general(
            active_low, scaled_error, (((0,), (0,)), ((), ())), preferred_element_type=jnp.float32
        )
        * hidden ** (-0.5)
    ).astype(jnp.bfloat16)
    backward = lax.dot_general(
        scaled_error, full_out, (((1,), (1,)), ((), ())), preferred_element_type=jnp.float32
    ) * hidden ** (-0.5)
    grad_before = pullback(backward)[0].astype(jnp.bfloat16)
    term_in = (
        lax.dot_general(
            grad_before, frames_here, (((0,), (0,)), ((), ())), preferred_element_type=jnp.float32
        )
        * model_width ** (-0.5)
    ).astype(jnp.bfloat16)
    return (term_in, term_out)


def body(student_frames, teacher_layers, mask_blocks, w_in, w_out, teacher_in, teacher_out):
    full_in, full_out = (
        lax.all_gather(w_in, "fsdp", axis=0, tiled=True),
        lax.all_gather(w_out, "fsdp", axis=0, tiled=True),
    )
    count_dp = lax.axis_size("dp")
    count_fsdp = lax.axis_size("fsdp")
    total_masked = count_dp * count_fsdp * mask_blocks.shape[1] * SPAN
    term_in, term_out = local_terms(
        student_frames, teacher_layers, mask_blocks[0], full_in, full_out, total_masked
    )
    summands = (term_in.astype(jnp.float32), term_out.astype(jnp.float32))
    shards = (
        lax.psum_scatter(summands[0], "fsdp", scatter_dimension=0, tiled=True),
        lax.psum_scatter(summands[1], "fsdp", scatter_dimension=0, tiled=True),
    )
    grad_in, grad_out = lax.psum((shards[0], shards[1]), "dp")
    ema_decay = 0.999
    new_in = ema_decay * teacher_in + (1.0 - ema_decay) * w_in.astype(jnp.float32)
    new_out = ema_decay * teacher_out + (1.0 - ema_decay) * w_out.astype(jnp.float32)
    return (grad_in, grad_out, new_in, new_out)


def solution(mesh):
    return jax.shard_map(
        body,
        mesh=mesh,
        in_specs=(
            P(("dp", "fsdp"), None),
            P(None, ("dp", "fsdp"), None),
            P(("dp", "fsdp"), None),
            P("fsdp", None),
            P("fsdp", None),
            P("fsdp", None),
            P("fsdp", None),
        ),
        out_specs=(P("fsdp", None), P("fsdp", None), P("fsdp", None), P("fsdp", None)),
        check_vma=False,
    )
```

profile of v0, /device:TPU:0, one launch (start us, length us, event | category | flops | bytes accessed | tf_op | source)
XLA Modules:
  0.0 185.0 jit_solution(17254358617561235314)
XLA Ops:
  7.2 0.0 reduce-scatter.3.cloned.1.call-start
  7.2 2.1 %convert_reduce_fusion = f32[2,1024]{1,0:T(2,128)S(1)} fusion(bf16[2,512,1024]{2,1,0:T(8,128)(2,1)} %param.8), kind=kLoop, calls=%fused_computation.1 | loop fusion | flops 2095104 | bytes 2105344 | tf_op jit(solution)/shard_map/reduce_sum | solution.py:15
  9.3 0.2 copy-done.1
  9.5 0.6 fusion.2
  10.1 0.6 fusion.3
  10.7 0.3 copy-done.3
  11.0 10.0 %all_gather.6 = bf16[384,1024]{1,0:T(8,128)(2,1)S(1)} all-gather(bf16[96,1024]{1,0:T(8,128)(2,1)S(1)} %copy-done.3), channel_id=1, replica_groups=mesh['dp'=8,'fsdp'=4] {'fsdp'}, dimensions={0}, use_global_device_ids=true | all-gather | bytes 983040 | tf_op jit(solution)/shard_map/all_gather | solution.py:61
  21.0 8.7 %all_gather.7 = bf16[384,1024]{1,0:T(8,128)(2,1)S(1)} all-gather(bf16[96,1024]{1,0:T(8,128)(2,1)S(1)} %copy-done.2), channel_id=1, replica_groups=mesh['dp'=8,'fsdp'=4] {'fsdp'}, dimensions={0}, use_global_device_ids=true | all-gather | bytes 983040 | tf_op jit(solution)/shard_map/all_gather | solution.py:62
  29.8 0.1 compare_reduce_fusion
  29.9 0.7 convolution_multiply_fusion.1
  30.6 1.9 %multiply_convert_fusion = bf16[512,1024]{1,0:T(8,128)(2,1)} fusion(f32[512,1024]{1,0:T(8,128)S(1)} %fusion.3, bf16[384,1024]{1,0:T(8,128)(2,1)S(1)} %all_gather.7, f32[512]{0:T(512)S(1)} %convert_element_type.37, f32[512,384]{1,0:T(8,128)S(1)} %convolution_multiply_fusion.1), kind=kOutput, calls=%fused_computation.6 | convolution fusion | flops 407568384 | bytes 4720640 | tf_op jit(solution)/shard_map/dot_general | solution.py:34
  32.5 4.0 %fusion.4 = f32[384,1024]{1,0:T(8,128)} fusion(bf16[512,1024]{1,0:T(8,128)(2,1)S(1)} %copy-done, f32[512,384]{1,0:T(8,128)S(1)} %convolution_multiply_fusion.1, bf16[512,1024]{1,0:T(8,128)(2,1)} %multiply_convert_fusion, bf16[384,1024]{1,0:T(8,128)(2,1)S(1)} %all_gather.7), kind=kOutput, calls=%fused_computation.9 | convolution fusion | flops 810614784 | bytes 5242880 | tf_op jit(solution)/shard_map/dot_general | solution.py:51
  36.5 0.0 reduce-scatter.3.cloned.1.call-update
  36.5 0.0 reduce-scatter.5.cloned.1.call-start
  36.5 3.1 %fusion.5 = f32[384,1024]{1,0:T(8,128)} fusion(bf16[512,1024]{1,0:T(8,128)(2,1)} %multiply_convert_fusion, f32[512,384]{1,0:T(8,128)S(1)} %convolution_multiply_fusion.1), kind=kOutput, calls=%fused_computation.10 | convolution fusion | flops 405602304 | bytes 3407872 | tf_op jit(solution)/shard_map/dot_general | solution.py:41
  39.6 0.0 reduce-scatter.5.cloned.1.call-update
  39.6 0.0 all-reduce.3.cloned.1.call-start
  39.7 26.0 %reduce-scatter.3.cloned.1.call-done = f32[96,1024]{1,0:T(8,128)} async-done(((f32[384,1024]{1,0:T(8,128)}), f32[96,1024]{1,0:T(8,128)}) %reduce-scatter.3.cloned.1.call-update) | async-done | bytes 393232 | tf_op jit(solution)/shard_map/reduce_scatter | solution.py:72
  65.7 30.9 %reduce-scatter.5.cloned.1.call-done = f32[96,1024]{1,0:T(8,128)} async-done(((f32[384,1024]{1,0:T(8,128)}), f32[96,1024]{1,0:T(8,128)}) %reduce-scatter.5.cloned.1.call-update) | async-done | bytes 393232 | tf_op jit(solution)/shard_map/reduce_scatter | solution.py:73
  96.6 0.8 multiply_add_fusion
  97.4 0.8 multiply_add_fusion.1
  98.2 76.7 %all-reduce.3.cloned.1.call-done = (f32[96,1024]{1,0:T(8,128)}, f32[96,1024]{1,0:T(8,128)}) async-done(((f32[96,1024]{1,0:T(8,128)}, f32[96,1024]{1,0:T(8,128)}), (f32[96,1024]{1,0:T(8,128)}, f32[96,1024]{1,0:T(8,128)})) %all-reduce.3.cloned.1.call-update) | async-done | bytes 786448 | tf_op jit(solution)/shard_map/psum | solution.py:75
  174.9 1.8 copy.13
  176.7 1.8 copy.14
  (17 shorter events, 0.1 us)
Async XLA Ops:
  7.2 22.7 %copy-start = (bf16[512,1024]{1,0:T(8,128)(2,1)S(1)}, bf16[512,1024]{1,0:T(8,128)(2,1)}, u32[]{:S(2)}) copy-start(bf16[512,1024]{1,0:T(8,128)(2,1)} %param.7) | copy-start | bytes 3145732
  7.2 2.3 %copy-start.1 = (bf16[2,512,1024]{2,1,0:T(8,128)(2,1)S(1)}, bf16[2,512,1024]{2,1,0:T(8,128)(2,1)}, u32[]{:S(2)}) copy-start(bf16[2,512,1024]{2,1,0:T(8,128)(2,1)} %param.8) | copy-start | bytes 6291460
  7.2 58.5 %reduce-scatter.3.cloned.1.call-start = ((), (), s32[]{:S(2)}) async-start(), calls=%async_computation.2 | async-start | bytes 1966080 | tf_op jit(solution)/shard_map/reduce_scatter | solution.py:72
  10.1 0.9 copy-start.3
  10.1 11.0 %copy-start.2 = (bf16[96,1024]{1,0:T(8,128)(2,1)S(1)}, bf16[96,1024]{1,0:T(8,128)(2,1)}, u32[]{:S(2)}) copy-start(bf16[96,1024]{1,0:T(8,128)(2,1)} %param.11) | copy-start | bytes 589828
  10.1 19.6 %copy-start.6 = (s32[1,32]{1,0:T(1,128)S(1)}, s32[1,32]{1,0:T(1,128)}, u32[]{:S(2)}) copy-start(s32[1,32]{1,0:T(1,128)} %param.9) | copy-start | bytes 388
  36.5 60.1 %reduce-scatter.5.cloned.1.call-start = ((), (), s32[]{:S(2)}) async-start(), calls=%async_computation.3 | async-start | bytes 1966080 | tf_op jit(solution)/shard_map/reduce_scatter | solution.py:73
  39.6 57.0 %copy-start.4 = (f32[96,1024]{1,0:T(8,128)S(1)}, f32[96,1024]{1,0:T(8,128)}, u32[]{:S(2)}) copy-start(f32[96,1024]{1,0:T(8,128)} %param.13) | copy-start | bytes 1179652
  39.6 57.8 %copy-start.5 = (f32[96,1024]{1,0:T(8,128)S(1)}, f32[96,1024]{1,0:T(8,128)}, u32[]{:S(2)}) copy-start(f32[96,1024]{1,0:T(8,128)} %param.12) | copy-start | bytes 1179652
  39.6 135.3 %all-reduce.3.cloned.1.call-start = ((), (), s32[]{:S(2)}) async-start(), calls=%async_computation.4 | async-start | bytes 1572864 | tf_op jit(solution)/shard_map/psum | solution.py:75
Sparse Core Ops, SparseCore 0:
  36.6 29.0 reduce-scatter.2
  68.4 28.1 reduce-scatter.4
  100.0 74.8 all-reduce.2
where the time goes:
time: 185 us
  waiting for transfers between devices  134 us (72%)
  blocking collectives  18.7 us (10%)
  between operations  13.8 us (7%)
  matrix products  9.64 us (5%)
  other arithmetic  4.97 us (3%)
  local copies, waits for them, and re-layouts  4.02 us (2%)
    psum x1, waiting for transfers between devices, body(): grad_in, grad_out = lax.psum((shards[0], shards[1]), 'dp')  76.7 us
    reduce_scatter x1, waiting for transfers between devices, body(): lax.psum_scatter(summands[1], 'fsdp', scatter_dimension=0, tiled=True)  30.9 us
    reduce_scatter x1, waiting for transfers between devices, body(): lax.psum_scatter(summands[0], 'fsdp', scatter_dimension=0, tiled=True)  26 us
    all_gather x1, blocking collectives, body(): lax.all_gather(w_in, 'fsdp', axis=0, tiled=True)  10 us
    all_gather x1, blocking collectives, body(): lax.all_gather(w_out, 'fsdp', axis=0, tiled=True)  8.71 us
    unnamed x16, local copies, waits for them, and re-layouts  4.02 us
    dot_general x1, matrix products, local_terms(): lax.dot_general(grad_before, frames_here, (((0,), (0,)), ((), ())), prefe...  3.97 us
  transfers between devices with their start and end apart: 3, of which 3 were waited for; matrix products, arithmetic and copies ran while one was open for 3% of the time, Pallas kernels for 0%

commit v1 on v0

--- a/solution.py
+++ b/solution.py
@@ -1,7 +1,13 @@
+import functools
+
 import jax
 import jax.numpy as jnp
 from jax import lax
+from jax.experimental import pallas as pl
+from jax.experimental.pallas import tpu as pltpu
 from jax.sharding import PartitionSpec as P
+
+MESH = pl.DeviceIdType.MESH
 
 SPAN = 8
 
@@ -56,7 +62,329 @@
     return (term_in, term_out)
 
 
+ROOT_2_PI = 0.7978845608028654
+CUBIC = 0.044715
+
+
+def head_kernel(
+    scale_error,
+    frames_hbm, layers_hbm, mask_ref, w_in_ref, w_out_ref,
+    grad_ref,
+    frames, layers, target, full_in, full_out, active_t, slope_t, error, grad_t,
+    term, pair_in, x_out, x_in, y_out, y_in, kept, half_kept, z_out, z_in, z_kept, whole,
+    local_sem, w_send, w_recv, g_send, g_recv,
+):
+    f = lax.axis_index("fsdp")
+    d = lax.axis_index("dp")
+    x, c = f // 2, f % 2
+    z, y = d // 2, d % 2
+    sibling = {"dp": d, "fsdp": 2 * x + (1 - c)}
+    x_peer = {"dp": d, "fsdp": 2 * (1 - x) + c}
+    y_peer = {"dp": 2 * z + (1 - y), "fsdp": f}
+    z_peers = [{"dp": 2 * ((z + j) % 4) + y, "fsdp": f} for j in (1, 2, 3)]
+    far = 2 * (1 - x) + c
+
+    loads = [
+        pltpu.make_async_copy(layers_hbm, layers, local_sem.at[0]),
+        pltpu.make_async_copy(frames_hbm, frames, local_sem.at[1]),
+        pltpu.make_async_copy(w_in_ref, full_in.at[f], local_sem.at[2]),
+        pltpu.make_async_copy(w_out_ref, full_out.at[f], local_sem.at[3]),
+    ]
+    for load in loads:
+        load.start()
+
+    barrier = pltpu.get_barrier_semaphore()
+    peers = [sibling, x_peer, y_peer] + z_peers
+    for peer in peers:
+        pl.semaphore_signal(barrier, inc=1, device_id=peer, device_id_type=MESH)
+    pl.semaphore_wait(barrier, len(peers))
+
+    pending = []
+
+    def remote(src, dst, send, recv, peer):
+        copy = pltpu.make_async_remote_copy(
+            src_ref=src, dst_ref=dst, send_sem=send, recv_sem=recv,
+            device_id=peer, device_id_type=MESH,
+        )
+        copy.start()
+        pending.append(copy)
+        return copy
+
+    shards = ((w_in_ref, full_in), (w_out_ref, full_out))
+    over_x, to_sibling = [], []
+    for k, (shard, full) in enumerate(shards):
+        over_x.append(remote(shard.at[y], full.at[f, y], w_send.at[k, 0], w_recv.at[k, 0], x_peer))
+    for k, (shard, full) in enumerate(shards):
+        to_sibling.append([remote(shard, full.at[f], w_send.at[k, 1], w_recv.at[k, 1], sibling)])
+
+    over_y = []
+
+    def forward_x(k):
+        full = shards[k][1]
+        over_x[k].wait_recv()
+        over_y.append(remote(full.at[far, y], full.at[far, y], w_send.at[k, 2], w_recv.at[k, 2], y_peer))
+        to_sibling[k].append(
+            remote(full.at[far, y], full.at[far, y], w_send.at[k, 3], w_recv.at[k, 3], sibling)
+        )
+
+    def forward_y(k):
+        full = shards[k][1]
+        over_y[k].wait_recv()
+        to_sibling[k].append(
+            remote(full.at[far, 1 - y], full.at[far, 1 - y], w_send.at[k, 4], w_recv.at[k, 4], sibling)
+        )
+
+    count, width = frames.shape
+    def targets(first, last):
+        for start in range(first, last, 128):
+            total = None
+            for layer in range(2):
+                v = layers[layer, :, start:start + 128].astype(jnp.float32)
+                center = v - jnp.mean(v, axis=0, keepdims=True)
+                spread = jnp.mean(center * center, axis=0, keepdims=True)
+                part = center * (0.5 / jnp.sqrt(spread + 1e-05))
+                total = part if total is None else total + part
+            target[:, start:start + 128] = total
+
+    loads[0].wait()
+    targets(0, width // 2)
+    forward_x(0)
+    targets(width // 2, 3 * width // 4)
+    forward_y(0)
+    forward_x(1)
+    targets(3 * width // 4, width)
+    block_of = lax.broadcasted_iota(jnp.int32, (count, mask_ref.shape[1]), 0) // SPAN
+    hits = jnp.where(block_of == mask_ref[...], 1.0, 0.0)
+    masked = jnp.max(hits, axis=1, keepdims=True)
+    loads[1].wait()
+    loads[2].wait()
+    for copy in to_sibling[0]:
+        copy.wait_recv()
+
+    hidden = 8 * full_in.shape[2]
+    rows = hidden // 8
+    in_all = full_in[...].reshape(hidden, width)
+    before = lax.dot_general(
+        in_all, frames[...], (((1,), (1,)), ((), ())), preferred_element_type=jnp.float32
+    ) * width ** (-0.5)
+    bend = jnp.tanh(ROOT_2_PI * (before + CUBIC * before * before * before))
+    active_t[...] = (before * (0.5 * (1.0 + bend))).astype(jnp.bfloat16)
+    slope_t[...] = 0.5 * (1.0 + bend) + (0.5 * ROOT_2_PI) * before * (1.0 - bend * bend) * (
+        1.0 + 3.0 * CUBIC * before * before
+    )
+
+    forward_y(1)
+    loads[3].wait()
+    for copy in to_sibling[1]:
+        copy.wait_recv()
+    active = active_t[...].T
+
+    half = width // 2
+
+    def errors(start):
+        for at in range(start, start + half, 256):
+            predicted = jnp.dot(
+                active, full_out[:, :, :, at:at + 256].reshape(hidden, 256),
+                preferred_element_type=jnp.float32,
+            ) * hidden ** (-0.5)
+            error[:, at:at + 256] = (
+                masked * (predicted - target[:, at:at + 256]) * scale_error
+            ).astype(jnp.bfloat16)
+
+    sent = {}
+
+    def send_pair(s, value):
+        value = value.astype(jnp.bfloat16)
+        for i in range(8):
+            term[s, i // 2, i % 2] = value[i * rows:(i + 1) * rows]
+        sent[s, "pair"] = [
+            remote(term.at[s, 2 * i + (1 - c)], pair_in.at[s, i], g_send.at[s, i], g_recv.at[s, i], sibling)
+            for i in range(2)
+        ]
+
+    def wide(value):
+        return value.astype(jnp.float32)
+
+    def send_x(s, ref):
+        return [remote(ref[0], ref[1], g_send.at[s, 2], g_recv.at[s, 2], x_peer)]
+
+    def send_y(s, ref):
+        return [remote(ref[0], ref[1], g_send.at[s, 3], g_recv.at[s, 3], y_peer)]
+
+    def arrived(s, name):
+        for copy in sent[s, name]:
+            copy.wait_recv()
+
+    def first(s):
+        arrived(s, "pair")
+        if s < 2:
+            x_out[s] = (wide(term[s, far]) + wide(pair_in[s, 1 - x])).astype(jnp.bfloat16)
+            sent[s, "first"] = send_x(s, (x_out.at[s], x_in.at[s]))
+            kept[s] = wide(term[s, f]) + wide(pair_in[s, x])
+        else:
+            for i in range(2):
+                y_out[s, i] = (
+                    wide(term[s, 2 * i + c, 1 - y]) + wide(pair_in[s, i, 1 - y])
+                ).astype(jnp.bfloat16)
+            sent[s, "first"] = send_y(s, (y_out.at[s], y_in.at[s]))
+            for i in range(2):
+                kept[s, i] = wide(term[s, 2 * i + c, y]) + wide(pair_in[s, i, y])
+
+    def second(s):
+        arrived(s, "first")
+        if s < 2:
+            y_out[s, 0] = (kept[s, 1 - y] + wide(x_in[s, 1 - y])).astype(jnp.bfloat16)
+            sent[s, "second"] = send_y(s, (y_out.at[s, 0], y_in.at[s, 0]))
+            half_kept[s] = kept[s, y] + wide(x_in[s, y])
+        else:
+            x_out[s, 0] = (kept[s, 1 - x] + wide(y_in[s, 1 - x])).astype(jnp.bfloat16)
+            sent[s, "second"] = send_x(s, (x_out.at[s, 0], x_in.at[s, 0]))
+            half_kept[s] = kept[s, x] + wide(y_in[s, x])
+
+    quarter = half // 4
+
+    def third(s):
+        arrived(s, "second")
+        total = half_kept[s] + wide(y_in[s, 0] if s < 2 else x_in[s, 0])
+        for q in range(4):
+            part = total[:, q * quarter:(q + 1) * quarter]
+            z_out[s, q] = part.astype(jnp.bfloat16)
+            z_kept[s, q] = part
+        sent[s, "third"] = [
+            remote(
+                z_out.at[s, (z + j) % 4], z_in.at[s, j - 1],
+                g_send.at[s, 3 + j], g_recv.at[s, 3 + j], z_peers[j - 1],
+            )
+            for j in (1, 2, 3)
+        ]
+
+    def fourth(s):
+        arrived(s, "third")
+        total = z_kept[s, z] + wide(z_in[s, 0]) + wide(z_in[s, 1]) + wide(z_in[s, 2])
+        whole[s, y, z] = total.astype(jnp.bfloat16)
+        sent[s, "fourth"] = [
+            remote(
+                whole.at[s, y, z], whole.at[s, y, z],
+                g_send.at[s, 6 + j], g_recv.at[s, 6 + j], z_peers[j - 1],
+            )
+            for j in (1, 2, 3)
+        ]
+
+    def fifth(s):
+        arrived(s, "fourth")
+        sent[s, "fifth"] = [
+            remote(whole.at[s, y], whole.at[s, y], g_send.at[s, 10], g_recv.at[s, 10], y_peer)
+        ]
+
+    def last(s):
+        arrived(s, "fifth")
+        for h in range(2):
+            for q in range(4):
+                at = (s % 2) * half + q * quarter
+                grad_ref[s // 2, h * rows:(h + 1) * rows, at:at + quarter] = whole[s, h, q]
+
+    for s in range(2):
+        at = s * half
+        errors(at)
+        send_pair(
+            s,
+            jnp.dot(active_t[...], error[:, at:at + half], preferred_element_type=jnp.float32)
+            * hidden ** (-0.5),
+        )
+    first(0)
+    backward = lax.dot_general(
+        full_out[...].reshape(hidden, width), error[...], (((1,), (1,)), ((), ())),
+        preferred_element_type=jnp.float32,
+    ) * hidden ** (-0.5)
+    grad_t[...] = (slope_t[...] * backward).astype(jnp.bfloat16)
+    first(1)
+    for s in range(2, 4):
+        at = (s - 2) * half
+        send_pair(
+            s,
+            jnp.dot(grad_t[...], frames[:, at:at + half], preferred_element_type=jnp.float32)
+            * width ** (-0.5),
+        )
+    first(2)
+    first(3)
+    for step in (second, third, fourth, fifth, last):
+        for s in (0, 2, 1, 3):
+            step(s)
+    for copy in pending:
+        copy.wait_send()
+
+
+def head_call(student_frames, teacher_layers, mask_blocks, w_in, w_out, scale_error):
+    count, width = student_frames.shape
+    shard = w_in.shape[0]
+    hidden = 4 * shard
+    rows, half, quarter = shard // 2, width // 2, width // 8
+    low, f32 = jnp.bfloat16, jnp.float32
+    anywhere = pl.BlockSpec(memory_space=pl.ANY)
+    inside = pl.BlockSpec(memory_space=pltpu.VMEM)
+    return pl.pallas_call(
+        functools.partial(head_kernel, scale_error),
+        out_shape=jax.ShapeDtypeStruct((2, shard, width), low),
+        in_specs=[anywhere, anywhere, inside, anywhere, anywhere],
+        out_specs=inside,
+        scratch_shapes=[
+            pltpu.VMEM((count, width), low),
+            pltpu.VMEM((2, count, width), low),
+            pltpu.VMEM((count, width), f32),
+            pltpu.VMEM((4, 2, rows, width), low),
+            pltpu.VMEM((4, 2, rows, width), low),
+            pltpu.VMEM((hidden, count), low),
+            pltpu.VMEM((hidden, count), f32),
+            pltpu.VMEM((count, width), low),
+            pltpu.VMEM((hidden, count), low),
+            pltpu.VMEM((4, 4, 2, rows, half), low),
+            pltpu.VMEM((4, 2, 2, rows, half), low),
+            pltpu.VMEM((4, 2, rows, half), low),
+            pltpu.VMEM((4, 2, rows, half), low),
+            pltpu.VMEM((4, 2, rows, half), low),
+            pltpu.VMEM((4, 2, rows, half), low),
+            pltpu.VMEM((4, 2, rows, half), f32),
+            pltpu.VMEM((4, rows, half), f32),
+            pltpu.VMEM((4, 4, rows, quarter), low),
+            pltpu.VMEM((4, 3, rows, quarter), low),
+            pltpu.VMEM((4, 4, rows, quarter), f32),
+            pltpu.VMEM((4, 2, 4, rows, quarter), low),
+            pltpu.SemaphoreType.DMA((4,)),
+            pltpu.SemaphoreType.DMA((2, 5)),
+            pltpu.SemaphoreType.DMA((2, 5)),
+            pltpu.SemaphoreType.DMA((4, 11)),
+            pltpu.SemaphoreType.DMA((4, 11)),
+        ],
+        compiler_params=pltpu.CompilerParams(
+            collective_id=0, has_side_effects=True, vmem_limit_bytes=48 * 1024 * 1024
+        ),
+        cost_estimate=pl.CostEstimate(
+            flops=10 * count * hidden * width,
+            bytes_accessed=6 * count * width + 4 * hidden * width,
+            transcendentals=count * hidden,
+        ),
+    )(
+        student_frames, teacher_layers, mask_blocks,
+        w_in.reshape(2, rows, width), w_out.reshape(2, rows, width),
+    )
+
+
+def averaged(w_in, w_out, teacher_in, teacher_out):
+    ema_decay = 0.999
+    new_in = ema_decay * teacher_in + (1.0 - ema_decay) * w_in.astype(jnp.float32)
+    new_out = ema_decay * teacher_out + (1.0 - ema_decay) * w_out.astype(jnp.float32)
+    return (new_in, new_out)
+
+
 def body(student_frames, teacher_layers, mask_blocks, w_in, w_out, teacher_in, teacher_out):
+    fused = lax.axis_size("fsdp") == 4 and lax.axis_size("dp") == 8
+    if fused:
+        total_masked = 32 * mask_blocks.shape[1] * SPAN
+        grads = head_call(
+            student_frames, teacher_layers, mask_blocks, w_in, w_out,
+            (4 * w_in.shape[0] / total_masked) ** 0.5,
+        ).astype(jnp.float32)
+        return (grads[1], grads[0]) + averaged(w_in, w_out, teacher_in, teacher_out)
     full_in, full_out = (
         lax.all_gather(w_in, "fsdp", axis=0, tiled=True),
         lax.all_gather(w_out, "fsdp", axis=0, tiled=True),
@@ -73,10 +401,7 @@
         lax.psum_scatter(summands[1], "fsdp", scatter_dimension=0, tiled=True),
     )
     grad_in, grad_out = lax.psum((shards[0], shards[1]), "dp")
-    ema_decay = 0.999
-    new_in = ema_decay * teacher_in + (1.0 - ema_decay) * w_in.astype(jnp.float32)
-    new_out = ema_decay * teacher_out + (1.0 - ema_decay) * w_out.astype(jnp.float32)
-    return (grad_in, grad_out, new_in, new_out)
+    return (grad_in, grad_out) + averaged(w_in, w_out, teacher_in, teacher_out)
 
 
 def solution(mesh):

time: 185 us -> 54.5 us (0.29)
  waiting for transfers between devices: 134 us -> 0 us
  Pallas kernels: 0 us -> 46 us
  blocking collectives: 18.7 us -> 0 us
  between operations: 13.8 us -> 0.68 us
  matrix products: 9.64 us -> 0 us
  other arithmetic: 4.97 us -> 1.1 us
  local copies, waits for them, and re-layouts: 4.02 us -> 6.48 us
    psum x1 -> x0, waiting for transfers between devices: 76.7 us -> none  [body(): grad_in, grad_out = lax.psum((shards[0], shards[1]), 'dp')]
    reduce_scatter x2 -> x0, waiting for transfers between devices: 56.9 us -> none  [the longest x1 30.9 us: body(): lax.psum_scatter(summands[1], 'fsdp', scatter_dimension=0, tiled=True)]
    pallas_call x0 -> x1, Pallas kernels: none -> 46 us  [head_call(): pl.pallas_call(functools.partial(head_kernel, scale_error), out_shape=jax...]
    all_gather x2 -> x0, blocking collectives: 18.7 us -> none  [the longest x1 10 us: body(): lax.all_gather(w_in, 'fsdp', axis=0, tiled=True)]
    dot_general x4 -> x0, matrix products: 9.64 us -> none  [the longest x1 3.97 us: local_terms(): lax.dot_general(grad_before, frames_here, (((0,), (0,)), ((), ())), prefe...]
    reduce_sum x3 -> x0, other arithmetic: 3.23 us -> none  [the longest x1 2.08 us: targets_of(): center = values - jnp.mean(values, axis=1, keepdims=True)]
    unnamed x16 -> x14, local copies, waits for them, and re-layouts: 4.02 us -> 5.55 us
  transfers between devices with their start and end apart: 3 -> 0, of which waited for: 3 -> 0; matrix products, arithmetic and copies ran while one was open for 3% -> 0% of each run, Pallas kernels for 0% -> 0%
where the time goes in v1:
time: 54.5 us; the launch traced here: 54.2 us
  Pallas kernels  46 us (84%)
  local copies, waits for them, and re-layouts  6.48 us (12%)
  other arithmetic  1.1 us (2%)
  between operations  0.68 us (1%)
    pallas_call x1, Pallas kernels, head_call(): pl.pallas_call(functools.partial(head_kernel, scale_error), out_shape=jax...  46 us
    unnamed x14, local copies, waits for them, and re-layouts  5.55 us

profile of v1, /device:TPU:0, one launch (start us, length us, event | category | flops | bytes accessed | tf_op | source)
XLA Modules:
  0.0 54.2 jit_solution(12731333452340893884)
XLA Ops:
  0.6 0.0 copy-start
  0.6 0.9 %copy-done = bf16[96,1024]{1,0:T(8,128)(2,1)S(1)} copy-done((bf16[96,1024]{1,0:T(8,128)(2,1)S(1)}, bf16[96,1024]{1,0:T(8,128)(2,1)}, u32[]{:S(2)}) %copy-start) | copy-done | bytes 196632
  1.6 0.0 copy-start.1
  1.6 0.9 %copy-done.1 = bf16[96,1024]{1,0:T(8,128)(2,1)S(1)} copy-done((bf16[96,1024]{1,0:T(8,128)(2,1)S(1)}, bf16[96,1024]{1,0:T(8,128)(2,1)}, u32[]{:S(2)}) %copy-start.1) | copy-done | bytes 196632
  2.5 0.0 copy-start.2
  2.5 1.6 %copy-done.2 = bf16[2,512,1024]{2,1,0:T(8,128)(2,1)S(1)} copy-done((bf16[2,512,1024]{2,1,0:T(8,128)(2,1)S(1)}, bf16[2,512,1024]{2,1,0:T(8,128)(2,1)}, u32[]{:S(2)}) %copy-start.2) | copy-done | bytes 2097176
  4.1 0.0 copy-start.3
  4.1 1.2 %copy-done.3 = bf16[512,1024]{1,0:T(8,128)(2,1)S(1)} copy-done((bf16[512,1024]{1,0:T(8,128)(2,1)S(1)}, bf16[512,1024]{1,0:T(8,128)(2,1)}, u32[]{:S(2)}) %copy-start.3) | copy-done | bytes 1048600
  5.3 0.0 copy-start.4
  5.3 0.7 %copy-done.4 = s32[1,32]{1,0:T(1,128)S(1)} copy-done((s32[1,32]{1,0:T(1,128)S(1)}, s32[1,32]{1,0:T(1,128)}, u32[]{:S(2)}) %copy-start.4) | copy-done | bytes 152
  6.0 46.0 %shard_map.102 = bf16[2,96,1024]{2,1,0:T(8,128)(2,1)S(1)} custom-call(bf16[512,1024]{1,0:T(8,128)(2,1)S(1)} %copy-done.3, bf16[2,512,1024]{2,1,0:T(8,128)(2,1)S(1)} %copy-done.2, s32[1,32]{1,0:T(1,128)S(1)} %copy-done.4, bf16[2,48,1024]{2,1,0:T(8,128)(2,1)S(1)} %bitcast.6, bf16[2,48,1024]{2,1,0:T(8,128)(2,1)S(1)} %bitcast.7), custom_call_target="tpu_custom_call" | custom-call | flops 2013265920 | bytes 4718592 | tf_op jit(solution)/shard_map/pallas_call | solution.py:325
  51.9 0.0 copy-start.5
  51.9 0.0 copy-start.6
  52.0 0.1 convert_element_type.9
  52.0 0.9 %slice_bitcast_fusion = (f32[96,1024]{1,0:T(8,128)}, f32[96,1024]{1,0:T(8,128)}) fusion(f32[2,96,1024]{2,1,0:T(8,128)S(1)} %convert_element_type.9), kind=kLoop, calls=%fused_computation | loop fusion | bytes 1572864 | tf_op jit(solution)/shard_map/squeeze | solution.py:387
  53.0 0.0 copy-done.5
  53.0 0.2 copy-done.6
  53.2 1.0 %multiply_add_fusion = (f32[96,1024]{1,0:T(8,128)}, f32[96,1024]{1,0:T(8,128)}) fusion(bf16[96,1024]{1,0:T(8,128)(2,1)S(1)} %copy-done.1, f32[96,1024]{1,0:T(8,128)S(1)} %copy-done.5, bf16[96,1024]{1,0:T(8,128)(2,1)S(1)} %copy-done, f32[96,1024]{1,0:T(8,128)S(1)} %copy-done.6), kind=kLoop, calls=%fused_computation.2 | loop fusion | flops 786432 | bytes 1966080 | tf_op jit(solution)/shard_map/add | solution.py:375
Async XLA Ops:
  0.6 0.9 %copy-start = (bf16[96,1024]{1,0:T(8,128)(2,1)S(1)}, bf16[96,1024]{1,0:T(8,128)(2,1)}, u32[]{:S(2)}) copy-start(bf16[96,1024]{1,0:T(8,128)(2,1)} %param.10) | copy-start | bytes 589828
  1.6 0.9 %copy-start.1 = (bf16[96,1024]{1,0:T(8,128)(2,1)S(1)}, bf16[96,1024]{1,0:T(8,128)(2,1)}, u32[]{:S(2)}) copy-start(bf16[96,1024]{1,0:T(8,128)(2,1)} %param.11) | copy-start | bytes 589828
  2.5 1.6 %copy-start.2 = (bf16[2,512,1024]{2,1,0:T(8,128)(2,1)S(1)}, bf16[2,512,1024]{2,1,0:T(8,128)(2,1)}, u32[]{:S(2)}) copy-start(bf16[2,512,1024]{2,1,0:T(8,128)(2,1)} %layers_hbm.1) | copy-start | bytes 6291460
  4.1 1.2 %copy-start.3 = (bf16[512,1024]{1,0:T(8,128)(2,1)S(1)}, bf16[512,1024]{1,0:T(8,128)(2,1)}, u32[]{:S(2)}) copy-start(bf16[512,1024]{1,0:T(8,128)(2,1)} %frames_hbm.1) | copy-start | bytes 3145732
  5.3 0.7 %copy-start.4 = (s32[1,32]{1,0:T(1,128)S(1)}, s32[1,32]{1,0:T(1,128)}, u32[]{:S(2)}) copy-start(s32[1,32]{1,0:T(1,128)} %mask_ref.1) | copy-start | bytes 388
  51.9 1.0 %copy-start.5 = (f32[96,1024]{1,0:T(8,128)S(1)}, f32[96,1024]{1,0:T(8,128)}, u32[]{:S(2)}) copy-start(f32[96,1024]{1,0:T(8,128)} %param.13) | copy-start | bytes 1179652
  51.9 1.2 %copy-start.6 = (f32[96,1024]{1,0:T(8,128)S(1)}, f32[96,1024]{1,0:T(8,128)}, u32[]{:S(2)}) copy-start(f32[96,1024]{1,0:T(8,128)} %param.12) | copy-start | bytes 1179652

commit v2 on v1

--- a/solution.py
+++ b/solution.py
@@ -82,6 +82,7 @@
     x_peer = {"dp": d, "fsdp": 2 * (1 - x) + c}
     y_peer = {"dp": 2 * z + (1 - y), "fsdp": f}
     z_peers = [{"dp": 2 * ((z + j) % 4) + y, "fsdp": f} for j in (1, 2, 3)]
+    across = [{"dp": 2 * ((z + j) % 4) + (1 - y), "fsdp": f} for j in (1, 2, 3)]
     far = 2 * (1 - x) + c
 
     loads = [
@@ -94,7 +95,7 @@
         load.start()
 
     barrier = pltpu.get_barrier_semaphore()
-    peers = [sibling, x_peer, y_peer] + z_peers
+    peers = [sibling, x_peer, y_peer] + z_peers + across
     for peer in peers:
         pl.semaphore_signal(barrier, inc=1, device_id=peer, device_id_type=MESH)
     pl.semaphore_wait(barrier, len(peers))
@@ -110,29 +111,15 @@
         pending.append(copy)
         return copy
 
-    shards = ((w_in_ref, full_in), (w_out_ref, full_out))
-    over_x, to_sibling = [], []
-    for k, (shard, full) in enumerate(shards):
-        over_x.append(remote(shard.at[y], full.at[f, y], w_send.at[k, 0], w_recv.at[k, 0], x_peer))
-    for k, (shard, full) in enumerate(shards):
-        to_sibling.append([remote(shard, full.at[f], w_send.at[k, 1], w_recv.at[k, 1], sibling)])
-
-    over_y = []
-
-    def forward_x(k):
-        full = shards[k][1]
-        over_x[k].wait_recv()
-        over_y.append(remote(full.at[far, y], full.at[far, y], w_send.at[k, 2], w_recv.at[k, 2], y_peer))
-        to_sibling[k].append(
-            remote(full.at[far, y], full.at[far, y], w_send.at[k, 3], w_recv.at[k, 3], sibling)
-        )
-
-    def forward_y(k):
-        full = shards[k][1]
-        over_y[k].wait_recv()
-        to_sibling[k].append(
-            remote(full.at[far, 1 - y], full.at[far, 1 - y], w_send.at[k, 4], w_recv.at[k, 4], sibling)
-        )
+    near = [
+        remote(w_in_ref, full_in.at[f], w_send.at[0, 0], w_recv.at[0, 0], sibling),
+        remote(w_out_ref, full_out.at[f], w_send.at[1, 0], w_recv.at[1, 0], sibling),
+    ]
+    out_x = remote(w_out_ref.at[y], full_out.at[f, y], w_send.at[1, 1], w_recv.at[1, 1], x_peer)
+    in_x = [
+        remote(w_in_ref.at[h], full_in.at[f, h], w_send.at[0, 1 + h], w_recv.at[0, 1 + h], x_peer)
+        for h in range(2)
+    ]
 
     count, width = frames.shape
     def targets(first, last):
@@ -148,17 +135,27 @@
 
     loads[0].wait()
     targets(0, width // 2)
-    forward_x(0)
+    out_x.wait_recv()
+    mine, other = full_out.at[far, y], full_out.at[far, 1 - y]
+    out_y = remote(mine, mine, w_send.at[1, 2], w_recv.at[1, 2], y_peer)
+    out_near = [remote(mine, mine, w_send.at[1, 3], w_recv.at[1, 3], sibling)]
     targets(width // 2, 3 * width // 4)
-    forward_y(0)
-    forward_x(1)
-    targets(3 * width // 4, width)
-    block_of = lax.broadcasted_iota(jnp.int32, (count, mask_ref.shape[1]), 0) // SPAN
-    hits = jnp.where(block_of == mask_ref[...], 1.0, 0.0)
-    masked = jnp.max(hits, axis=1, keepdims=True)
+    in_near = []
+    for h in range(2):
+        in_x[h].wait_recv()
+        piece = full_in.at[far, h]
+        in_near.append(remote(piece, piece, w_send.at[0, 3 + h], w_recv.at[0, 3 + h], sibling))
+        if h == 0:
+            targets(3 * width // 4, width)
+            block_of = lax.broadcasted_iota(jnp.int32, (count, mask_ref.shape[1]), 0) // SPAN
+            hits = jnp.where(block_of == mask_ref[...], 1.0, 0.0)
+            masked = jnp.max(hits, axis=1, keepdims=True)
+    out_y.wait_recv()
+    out_near.append(remote(other, other, w_send.at[1, 4], w_recv.at[1, 4], sibling))
     loads[1].wait()
     loads[2].wait()
-    for copy in to_sibling[0]:
+    near[0].wait_recv()
+    for copy in in_near:
         copy.wait_recv()
 
     hidden = 8 * full_in.shape[2]
@@ -173,9 +170,9 @@
         1.0 + 3.0 * CUBIC * before * before
     )
 
-    forward_y(1)
     loads[3].wait()
-    for copy in to_sibling[1]:
+    near[1].wait_recv()
+    for copy in out_near:
         copy.wait_recv()
     active = active_t[...].T
 
@@ -217,7 +214,7 @@
 
     def first(s):
         arrived(s, "pair")
-        if s < 2:
+        if s % 2 == 0:
             x_out[s] = (wide(term[s, far]) + wide(pair_in[s, 1 - x])).astype(jnp.bfloat16)
             sent[s, "first"] = send_x(s, (x_out.at[s], x_in.at[s]))
             kept[s] = wide(term[s, f]) + wide(pair_in[s, x])
@@ -232,7 +229,7 @@
 
     def second(s):
         arrived(s, "first")
-        if s < 2:
+        if s % 2 == 0:
             y_out[s, 0] = (kept[s, 1 - y] + wide(x_in[s, 1 - y])).astype(jnp.bfloat16)
             sent[s, "second"] = send_y(s, (y_out.at[s, 0], y_in.at[s, 0]))
             half_kept[s] = kept[s, y] + wide(x_in[s, y])
@@ -245,7 +242,7 @@
 
     def third(s):
         arrived(s, "second")
-        total = half_kept[s] + wide(y_in[s, 0] if s < 2 else x_in[s, 0])
+        total = half_kept[s] + wide(y_in[s, 0] if s % 2 == 0 else x_in[s, 0])
         for q in range(4):
             part = total[:, q * quarter:(q + 1) * quarter]
             z_out[s, q] = part.astype(jnp.bfloat16)
@@ -269,9 +266,19 @@
             )
             for j in (1, 2, 3)
         ]
+        if s >= 2:
+            sent[s, "fifth"] = [
+                remote(
+                    whole.at[s, y, z], whole.at[s, y, z],
+                    g_send.at[s, 10 + j], g_recv.at[s, 10 + j], ([y_peer] + across)[j],
+                )
+                for j in range(4)
+            ]
 
     def fifth(s):
         arrived(s, "fourth")
+        if s >= 2:
+            return
         sent[s, "fifth"] = [
             remote(whole.at[s, y], whole.at[s, y], g_send.at[s, 10], g_recv.at[s, 10], y_peer)
         ]
@@ -308,7 +315,7 @@
     first(2)
     first(3)
     for step in (second, third, fourth, fifth, last):
-        for s in (0, 2, 1, 3):
+        for s in range(4):
             step(s)
     for copy in pending:
         copy.wait_send()
@@ -352,11 +359,11 @@
             pltpu.SemaphoreType.DMA((4,)),
             pltpu.SemaphoreType.DMA((2, 5)),
             pltpu.SemaphoreType.DMA((2, 5)),
-            pltpu.SemaphoreType.DMA((4, 11)),
-            pltpu.SemaphoreType.DMA((4, 11)),
+            pltpu.SemaphoreType.DMA((4, 14)),
+            pltpu.SemaphoreType.DMA((4, 14)),
         ],
         compiler_params=pltpu.CompilerParams(
-            collective_id=0, has_side_effects=True, vmem_limit_bytes=48 * 1024 * 1024
+            collective_id=0, has_side_effects=True, vmem_limit_bytes=63 * 1024 * 1024
         ),
         cost_estimate=pl.CostEstimate(
             flops=10 * count * hidden * width,

time: 54.5 us -> 45.4 us (0.83)
  local copies, waits for them, and re-layouts: 6.48 us -> 0.96 us
  Pallas kernels: 46 us -> 41.4 us
  other arithmetic: 1.1 us -> 2.17 us
    unnamed x14 -> x8, local copies, waits for them, and re-layouts: 5.55 us -> 0.03 us
    pallas_call x1, Pallas kernels: 46 us -> 41.4 us  [head_call(): pl.pallas_call(functools.partial(head_kernel, scale_error), out_shape=jax...]
    convert_element_type x1, other arithmetic: 0.07 us -> 1.15 us  [body(): grads = head_call(student_frames, teacher_layers, mask_blocks, w_in, w_ou...]
where the time goes in v2:
time: 45.4 us; the launch traced here: 45.2 us
  Pallas kernels  41.4 us (91%)
  other arithmetic  2.17 us (5%)
  local copies, waits for them, and re-layouts  0.96 us (2%)
  between operations  0.69 us (2%)
    pallas_call x1, Pallas kernels, head_call(): pl.pallas_call(functools.partial(head_kernel, scale_error), out_shape=jax...  41.4 us
    convert_element_type x1, other arithmetic, body(): grads = head_call(student_frames, teacher_layers, mask_blocks, w_in, w_ou...  1.15 us
    add x1, other arithmetic, averaged(): ema_decay * teacher_out + (1.0 - ema_decay) * w_out.astype(jnp.float32)  1.02 us
    squeeze x1, local copies, waits for them, and re-layouts, body(): return (grads[1], grads[0]) + averaged(w_in, w_out, teacher_in, teacher_out)  0.93 us

profile of v2, /device:TPU:0, one launch (start us, length us, event | category | flops | bytes accessed | tf_op | source)
XLA Modules:
  0.0 45.2 jit_solution(5436078572456914400)
XLA Ops:
  0.6 41.4 %shard_map.102 = bf16[2,96,1024]{2,1,0:T(8,128)(2,1)} custom-call(bf16[512,1024]{1,0:T(8,128)(2,1)} %frames_hbm.1, bf16[2,512,1024]{2,1,0:T(8,128)(2,1)} %layers_hbm.1, s32[1,32]{1,0:T(1,128)} %mask_ref.1, bf16[2,48,1024]{2,1,0:T(8,128)(2,1)} %bitcast.6, bf16[2,48,1024]{2,1,0:T(8,128)(2,1)} %bitcast.7), custom_call_target="tpu_custom_call" | custom-call | flops 2013265920 | bytes 4718592 | tf_op jit(solution)/shard_map/pallas_call | solution.py:332
  42.0 0.0 copy-start
  42.0 0.0 copy-start.1
  42.1 0.0 copy-start.2
  42.1 0.0 copy-start.3
  42.1 1.2 %convert_element_type.9 = f32[2,96,1024]{2,1,0:T(8,128)S(1)} convert(bf16[2,96,1024]{2,1,0:T(8,128)(2,1)} %shard_map.102) | non-fusion elementwise | flops 196608 | bytes 1179648 | tf_op jit(solution)/shard_map/convert_element_type | solution.py:393
  43.2 0.9 %slice_bitcast_fusion = (f32[96,1024]{1,0:T(8,128)}, f32[96,1024]{1,0:T(8,128)}) fusion(f32[2,96,1024]{2,1,0:T(8,128)S(1)} %convert_element_type.9), kind=kLoop, calls=%fused_computation | loop fusion | bytes 1572864 | tf_op jit(solution)/shard_map/squeeze | solution.py:394
  44.2 0.0 copy-done
  44.2 0.0 copy-done.1
  44.2 0.0 copy-done.2
  44.2 0.0 copy-done.3
  44.2 1.0 %multiply_add_fusion = (f32[96,1024]{1,0:T(8,128)}, f32[96,1024]{1,0:T(8,128)}) fusion(bf16[96,1024]{1,0:T(8,128)(2,1)S(1)} %copy-done.3, f32[96,1024]{1,0:T(8,128)S(1)} %copy-done, bf16[96,1024]{1,0:T(8,128)(2,1)S(1)} %copy-done.2, f32[96,1024]{1,0:T(8,128)S(1)} %copy-done.1), kind=kLoop, calls=%fused_computation.2 | loop fusion | flops 786432 | bytes 1966080 | tf_op jit(solution)/shard_map/add | solution.py:382
Async XLA Ops:
  42.0 2.1 %copy-start = (f32[96,1024]{1,0:T(8,128)S(1)}, f32[96,1024]{1,0:T(8,128)}, u32[]{:S(2)}) copy-start(f32[96,1024]{1,0:T(8,128)} %param.13) | copy-start | bytes 1179652
  42.0 2.1 %copy-start.1 = (f32[96,1024]{1,0:T(8,128)S(1)}, f32[96,1024]{1,0:T(8,128)}, u32[]{:S(2)}) copy-start(f32[96,1024]{1,0:T(8,128)} %param.12) | copy-start | bytes 1179652
  42.1 2.1 %copy-start.2 = (bf16[96,1024]{1,0:T(8,128)(2,1)S(1)}, bf16[96,1024]{1,0:T(8,128)(2,1)}, u32[]{:S(2)}) copy-start(bf16[96,1024]{1,0:T(8,128)(2,1)} %param.10) | copy-start | bytes 589828
  42.1 2.1 %copy-start.3 = (bf16[96,1024]{1,0:T(8,128)(2,1)S(1)}, bf16[96,1024]{1,0:T(8,128)(2,1)}, u32[]{:S(2)}) copy-start(bf16[96,1024]{1,0:T(8,128)(2,1)} %param.11) | copy-start | bytes 589828

commit v3 on v2

--- a/solution.py
+++ b/solution.py
@@ -363,7 +363,7 @@
             pltpu.SemaphoreType.DMA((4, 14)),
         ],
         compiler_params=pltpu.CompilerParams(
-            collective_id=0, has_side_effects=True, vmem_limit_bytes=63 * 1024 * 1024
+            collective_id=0, has_side_effects=True, vmem_limit_bytes=62 * 1024 * 1024
         ),
         cost_estimate=pl.CostEstimate(
             flops=10 * count * hidden * width,
@@ -376,6 +376,24 @@
     )
 
 
+def finish_kernel(grads, w_in, w_out, teacher_in, teacher_out, grad_in, grad_out, new_in, new_out):
+    grad_in[...] = grads[1].astype(jnp.float32)
+    grad_out[...] = grads[0].astype(jnp.float32)
+    new_in[...], new_out[...] = averaged(w_in[...], w_out[...], teacher_in[...], teacher_out[...])
+
+
+def finish_call(grads, w_in, w_out, teacher_in, teacher_out):
+    shape = jax.ShapeDtypeStruct(teacher_in.shape, jnp.float32)
+    inside = pl.BlockSpec(memory_space=pltpu.VMEM)
+    return pl.pallas_call(
+        finish_kernel,
+        out_shape=[shape] * 4,
+        in_specs=[inside] * 5,
+        out_specs=[inside] * 4,
+        compiler_params=pltpu.CompilerParams(vmem_limit_bytes=16 * 1024 * 1024),
+    )(grads, w_in, w_out, teacher_in, teacher_out)
+
+
 def averaged(w_in, w_out, teacher_in, teacher_out):
     ema_decay = 0.999
     new_in = ema_decay * teacher_in + (1.0 - ema_decay) * w_in.astype(jnp.float32)
@@ -387,11 +405,11 @@
     fused = lax.axis_size("fsdp") == 4 and lax.axis_size("dp") == 8
     if fused:
         total_masked = 32 * mask_blocks.shape[1] * SPAN
-        grads = head_call(
+        low_grads = head_call(
             student_frames, teacher_layers, mask_blocks, w_in, w_out,
             (4 * w_in.shape[0] / total_masked) ** 0.5,
-        ).astype(jnp.float32)
-        return (grads[1], grads[0]) + averaged(w_in, w_out, teacher_in, teacher_out)
+        )
+        return tuple(finish_call(low_grads, w_in, w_out, teacher_in, teacher_out))
     full_in, full_out = (
         lax.all_gather(w_in, "fsdp", axis=0, tiled=True),
         lax.all_gather(w_out, "fsdp", axis=0, tiled=True),

time: 45.4 us -> 44.5 us (0.980)
  other arithmetic: 2.17 us -> 0 us
  Pallas kernels: 41.4 us -> 42.6 us
    pallas_call x0 -> x1, Pallas kernels: none -> 1.16 us  [finish_call(): pl.pallas_call(finish_kernel, out_shape=[shape] * 4, in_specs=[inside] *...]
    convert_element_type x1 -> x0, other arithmetic: 1.15 us -> none  [body(): grads = head_call(student_frames, teacher_layers, mask_blocks, w_in, w_ou...]
    add x1 -> x0, other arithmetic: 1.02 us -> none  [averaged(): ema_decay * teacher_out + (1.0 - ema_decay) * w_out.astype(jnp.float32)]
    unnamed x8 -> x10, local copies, waits for them, and re-layouts: 0.03 us -> 1.01 us
    squeeze x1 -> x0, local copies, waits for them, and re-layouts: 0.93 us -> none  [body(): return (grads[1], grads[0]) + averaged(w_in, w_out, teacher_in, teacher_out)]
where the time goes in v3:
time: 44.5 us; the launch traced here: 44.4 us
  Pallas kernels  42.6 us (96%)
  local copies, waits for them, and re-layouts  1.01 us (2%)
  between operations  0.71 us (2%)
    pallas_call x1, Pallas kernels, head_call(): pl.pallas_call(functools.partial(head_kernel, scale_error), out_shape=jax...  41.5 us
    pallas_call x1, Pallas kernels, finish_call(): pl.pallas_call(finish_kernel, out_shape=[shape] * 4, in_specs=[inside] *...  1.16 us
    unnamed x10, local copies, waits for them, and re-layouts  1.01 us

profile of v3, /device:TPU:0, one launch (start us, length us, event | category | flops | bytes accessed | tf_op | source)
XLA Modules:
  0.0 44.4 jit_solution(3718091699588903195)
XLA Ops:
  0.6 0.0 copy-start
  0.6 0.0 copy-start.1
  0.7 0.0 copy-start.3
  0.7 0.0 copy-start.4
  0.7 41.5 %shard_map.102.grads = bf16[2,96,1024]{2,1,0:T(8,128)(2,1)} custom-call(bf16[512,1024]{1,0:T(8,128)(2,1)} %frames_hbm.1, bf16[2,512,1024]{2,1,0:T(8,128)(2,1)} %layers_hbm.1, s32[1,32]{1,0:T(1,128)} %mask_ref.1, bf16[2,48,1024]{2,1,0:T(8,128)(2,1)} %bitcast.2, bf16[2,48,1024]{2,1,0:T(8,128)(2,1)} %bitcast.3), custom_call_target="tpu_custom_call" | custom-call | flops 2013265920 | bytes 4718592 | tf_op jit(solution)/shard_map/pallas_call | solution.py:332
  42.2 0.0 copy-done
  42.2 0.0 copy-done.1
  42.2 0.0 copy-done.3
  42.2 0.0 copy-done.4
  42.2 0.0 copy-start.2
  42.2 1.0 %copy-done.2 = bf16[2,96,1024]{2,1,0:T(8,128)(2,1)S(1)} copy-done((bf16[2,96,1024]{2,1,0:T(8,128)(2,1)S(1)}, bf16[2,96,1024]{2,1,0:T(8,128)(2,1)}, u32[]{:S(2)}) %copy-start.2) | copy-done | bytes 393240
  43.2 1.2 %shard_map.103 = (f32[96,1024]{1,0:T(8,128)}, f32[96,1024]{1,0:T(8,128)}, f32[96,1024]{1,0:T(8,128)}, f32[96,1024]{1,0:T(8,128)}) custom-call(bf16[2,96,1024]{2,1,0:T(8,128)(2,1)S(1)} %copy-done.2, bf16[96,1024]{1,0:T(8,128)(2,1)S(1)} %copy-done.3, bf16[96,1024]{1,0:T(8,128)(2,1)S(1)} %copy-done.4, f32[96,1024]{1,0:T(8,128)S(1)} %copy-done, ...), custom_call_target="tpu_custom_call" | custom-call | tf_op jit(solution)/shard_map/pallas_call | solution.py:388
Async XLA Ops:
  0.6 41.5 %copy-start = (f32[96,1024]{1,0:T(8,128)S(1)}, f32[96,1024]{1,0:T(8,128)}, u32[]{:S(2)}) copy-start(f32[96,1024]{1,0:T(8,128)} %teacher_in.1) | copy-start | bytes 1179652
  0.6 41.5 %copy-start.1 = (f32[96,1024]{1,0:T(8,128)S(1)}, f32[96,1024]{1,0:T(8,128)}, u32[]{:S(2)}) copy-start(f32[96,1024]{1,0:T(8,128)} %teacher_out.1) | copy-start | bytes 1179652
  0.7 41.5 %copy-start.3 = (bf16[96,1024]{1,0:T(8,128)(2,1)S(1)}, bf16[96,1024]{1,0:T(8,128)(2,1)}, u32[]{:S(2)}) copy-start(bf16[96,1024]{1,0:T(8,128)(2,1)} %w_in.1) | copy-start | bytes 589828
  0.7 41.5 %copy-start.4 = (bf16[96,1024]{1,0:T(8,128)(2,1)S(1)}, bf16[96,1024]{1,0:T(8,128)(2,1)}, u32[]{:S(2)}) copy-start(bf16[96,1024]{1,0:T(8,128)(2,1)} %w_out.1) | copy-start | bytes 589828
  42.2 1.0 %copy-start.2 = (bf16[2,96,1024]{2,1,0:T(8,128)(2,1)S(1)}, bf16[2,96,1024]{2,1,0:T(8,128)(2,1)}, u32[]{:S(2)}) copy-start(bf16[2,96,1024]{2,1,0:T(8,128)(2,1)} %shard_map.102.grads) | copy-start | bytes 1179652
